TPU v7x, 256 devices: a whole 4x4x8 slice. The times are simulated.
256 devices in a mesh: dp: 32 (over z, x), tensor: 8 (over y, core).
Axes of the slice: x: 4, y: 4, z: 8, core: 2. Of those that a mesh axis runs over, the one named last changes fastest.
Arguments:
- gate_grad: bfloat16 [32, 256, 14336], P('dp', None, 'tensor'), may hold values from -6 to 6
- up_grad: bfloat16 [32, 256, 14336], P('dp', None, 'tensor'), may hold values from -6 to 6
- gate_error: float32 [32, 256, 14336], P('dp', None, 'tensor'), may hold values from -4 to 4
- up_error: float32 [32, 256, 14336], P('dp', None, 'tensor'), may hold values from -4 to 4
- gate_q: float32 [14336, 32], P('tensor'), may hold values from -6 to 6
- up_q: float32 [14336, 32], P('tensor'), may hold values from -6 to 6
Outputs:
- gate_sum: bfloat16 [256, 14336], P(None, 'tensor')
- up_sum: bfloat16 [256, 14336], P(None, 'tensor')
- gate_next_q: float32 [14336, 32], P('tensor')
- up_next_q: float32 [14336, 32], P('tensor')
- gate_new_error: float32 [32, 256, 14336], P('dp', None, 'tensor')
- up_new_error: float32 [32, 256, 14336], P('dp', None, 'tensor')
All inputs are finite; a program needn't handle non-finite values.
Results may differ from a plain program's by a relative error of at most 0.0011.
Values sent between devices are 32-bit elements; how exact they have to be, the bound alone decides.
A program may use at most 64 MiB of HBM per device.

v0:
```python
import jax
import jax.numpy as jnp
from jax import lax
from jax.sharding import PartitionSpec as P


def orthogonal(left):
    gram = jnp.dot(left.T, left, precision=lax.Precision.HIGHEST)
    factor = jnp.linalg.cholesky(gram)
    return lax.linalg.triangular_solve(factor, left, left_side=False, lower=True, transpose_a=True)


def shards(gate_grad, up_grad, gate_error, up_error, gate_q, up_q):
    gate_full = gate_grad[0].astype(jnp.float32) + gate_error[0]
    up_full = up_grad[0].astype(jnp.float32) + up_error[0]
    gate_part = jnp.dot(gate_full, gate_q, precision=lax.Precision.HIGHEST)
    up_part = jnp.dot(up_full, up_q, precision=lax.Precision.HIGHEST)
    gate_mid, up_mid = lax.psum((gate_part, up_part), "tensor")
    gate_left, up_left = lax.psum((gate_mid, up_mid), "dp")
    gate_ortho = orthogonal(gate_left)
    up_ortho = orthogonal(up_left)
    gate_own = jnp.dot(gate_full.T, gate_ortho, precision=lax.Precision.HIGHEST)
    up_own = jnp.dot(up_full.T, up_ortho, precision=lax.Precision.HIGHEST)
    gate_new = gate_full - jnp.dot(gate_ortho, gate_own.T, precision=lax.Precision.HIGHEST)
    up_new = up_full - jnp.dot(up_ortho, up_own.T, precision=lax.Precision.HIGHEST)
    gate_next, up_next = lax.psum((gate_own, up_own), "dp")
    gate_sum = jnp.dot(gate_ortho, gate_next.T, precision=lax.Precision.HIGHEST).astype(
        jnp.bfloat16
    )
    up_sum = jnp.dot(up_ortho, up_next.T, precision=lax.Precision.HIGHEST).astype(jnp.bfloat16)
    return (gate_sum, up_sum, gate_next, up_next, gate_new[None], up_new[None])


def solution(mesh):
    in_specs = (
        P("dp", None, "tensor"),
        P("dp", None, "tensor"),
        P("dp", None, "tensor"),
        P("dp", None, "tensor"),
        P("tensor", None),
        P("tensor", None),
    )
    out_specs = (
        P(None, "tensor"),
        P(None, "tensor"),
        P("tensor", None),
        P("tensor", None),
        P("dp", None, "tensor"),
        P("dp", None, "tensor"),
    )
    return jax.shard_map(shards, mesh=mesh, in_specs=in_specs, out_specs=out_specs, check_vma=False)
```

profile of v0, /device:TPU:8, one launch (start us, length us, event | category | flops | bytes accessed | tf_op | source)
XLA Modules:
  0.0 417.3 jit_solution(13092592950466530955)
XLA Ops:
  7.2 0.0 all-reduce.11.cloned.1.call-start
  7.3 0.9 copy-done
  8.1 4.1 fusion.8
  12.2 2.3 fusion.4
  14.5 0.0 all-reduce.7.cloned.1.call-start
  14.5 64.8 %all-reduce.11.cloned.1.call-done = (f32[256,32]{0,1:T(8,128)}, f32[256,32]{0,1:T(8,128)}) async-done(((f32[256,32]{0,1:T(8,128)}, f32[256,32]{0,1:T(8,128)}), (f32[256,32]{0,1:T(8,128)}, f32[256,32]{0,1:T(8,128)})) %all-reduce.11.cloned.1.call-update) | async-done | bytes 65552 | tf_op jit(solution)/shard_map/psum | solution.py:18
  79.4 0.0 all-reduce.7.cloned.1.call-update
  79.4 144.2 %all-reduce.7.cloned.1.call-done = (f32[256,32]{0,1:T(8,128)}, f32[256,32]{0,1:T(8,128)}) async-done(((f32[256,32]{0,1:T(8,128)}, f32[256,32]{0,1:T(8,128)}), (f32[256,32]{0,1:T(8,128)}, f32[256,32]{0,1:T(8,128)})) %all-reduce.7.cloned.1.call-update) | async-done | bytes 65552 | tf_op jit(solution)/shard_map/psum | solution.py:19
  223.6 1.0 fusion.16
  224.6 1.0 fusion.17
  225.6 0.1 copy.13
  225.7 2.9 cholesky.55
  228.7 0.6 compare_reduce_fusion
  229.3 0.7 fusion.11
  230.0 2.4 custom-call.7
  232.4 1.0 convolution_bitcast_fusion
  233.4 0.1 copy.12
  233.5 2.9 cholesky.44
  236.4 0.6 compare_reduce_fusion.1
  237.1 0.7 fusion.10
  237.7 2.4 custom-call.6
  240.2 1.0 convolution_bitcast_fusion.1
  241.2 3.0 fusion.6
  244.2 1.3 fusion.2
  245.5 2.9 fusion.1
  248.4 2.9 fusion
  251.3 0.7 all-reduce.9.cloned.1.call-update
  252.0 150.3 %all-reduce.9.cloned.1.call-done = (f32[1792,32]{0,1:T(8,128)}, f32[1792,32]{0,1:T(8,128)}) async-done(((f32[1792,32]{0,1:T(8,128)}, f32[1792,32]{0,1:T(8,128)}), (f32[1792,32]{0,1:T(8,128)}, f32[1792,32]{0,1:T(8,128)})) %all-reduce.9.cloned.1.call-update) | async-done | bytes 458768 | tf_op jit(solution)/shard_map/psum | solution.py:26
  402.4 3.6 convolution_convert_fusion.1
  405.9 3.5 convolution_convert_fusion
  409.4 0.7 copy.20
  410.1 0.7 copy.21
  (25 shorter events, 0.1 us)
Async XLA Ops:
  7.2 0.9 copy-start
  7.2 5.0 %copy-start.1 = (f32[1,256,1792]{2,1,0:T(8,128)S(1)}, f32[1,256,1792]{2,1,0:T(8,128)}, u32[]{:S(2)}) copy-start(f32[1,256,1792]{2,1,0:T(8,128)} %param.12) | copy-start | bytes 5505028
  7.2 5.0 %copy-start.3 = (bf16[1,256,1792]{2,1,0:T(8,128)(2,1)S(1)}, bf16[1,256,1792]{2,1,0:T(8,128)(2,1)}, u32[]{:S(2)}) copy-start(bf16[1,256,1792]{2,1,0:T(8,128)(2,1)} %param.10) | copy-start | bytes 2752516
  7.2 5.0 %copy-start.9 = (f32[1792,32]{0,1:T(8,128)S(1)}, f32[1792,32]{0,1:T(8,128)}, u32[]{:S(2)}) copy-start(f32[1792,32]{0,1:T(8,128)} %param.14) | copy-start | bytes 688132
  7.2 72.2 %all-reduce.11.cloned.1.call-start = ((), (), s32[]{:S(2)}) async-start(), calls=%async_computation.2 | async-start | bytes 131072 | tf_op jit(solution)/shard_map/psum | solution.py:18
  14.5 209.1 %all-reduce.7.cloned.1.call-start = ((), (), s32[]{:S(2)}) async-start(), calls=%async_computation | async-start | bytes 131072 | tf_op jit(solution)/shard_map/psum | solution.py:19
  244.2 4.2 %copy-start.5 = (f32[1792,32]{0,1:T(8,128)}, f32[1792,32]{0,1:T(8,128)S(1)}, u32[]{:S(2)}) copy-start(f32[1792,32]{0,1:T(8,128)S(1)} %fusion.6) | copy-start | bytes 688132
  245.5 2.9 copy-start.6
  245.5 2.9 copy-start.2
  245.5 2.9 copy-start.4
  251.3 151.1 %all-reduce.9.cloned.1.call-start = ((), (), s32[]{:S(2)}) async-start(), calls=%async_computation.1 | async-start | bytes 917504 | tf_op jit(solution)/shard_map/psum | solution.py:26
  402.3 7.1 %copy-start.8 = (f32[1792,32]{0,1:T(8,128)S(1)}, f32[1792,32]{0,1:T(8,128)}, u32[]{:S(2)}) copy-start(f32[1792,32]{0,1:T(8,128)} %get-tuple-element.16) | copy-start | bytes 688132
  402.3 7.8 %copy-start.7 = (f32[1792,32]{0,1:T(8,128)S(1)}, f32[1792,32]{0,1:T(8,128)}, u32[]{:S(2)}) copy-start(f32[1792,32]{0,1:T(8,128)} %get-tuple-element.17) | copy-start | bytes 688132
Sparse Core Ops, SparseCore 0:
  14.6 64.7 all-reduce.10
  83.3 140.2 all-reduce.6
  256.5 145.7 all-reduce.8
where the time goes:
time: 418 us; the launch traced here: 417 us
  waiting for transfers between devices  360 us (86%)
  matrix products  27.4 us (7%)
  between operations  13.9 us (3%)
  other arithmetic  13.4 us (3%)
    psum x1, waiting for transfers between devices, shards(): gate_next, up_next = lax.psum((gate_own, up_own), 'dp')  150 us
    psum x1, waiting for transfers between devices, shards(): gate_left, up_left = lax.psum((gate_mid, up_mid), 'dp')  144 us
    psum x1, waiting for transfers between devices, shards(): gate_mid, up_mid = lax.psum((gate_part, up_part), 'tensor')  64.8 us
  transfers between devices with their start and end apart: 3, of which 3 were waited for; matrix products, arithmetic and copies ran while one was open for 0% of the time, Pallas kernels for 0%

commit v1 on v0

v1 whole, which is shorter than its diff:
```python
import functools

import jax
import jax.numpy as jnp
from jax import lax
from jax.experimental import pallas as pl
from jax.experimental.pallas import tpu as pltpu
from jax.sharding import PartitionSpec as P

MESH = pl.DeviceIdType.MESH
F32, BF16 = jnp.float32, jnp.bfloat16
HIGHEST = lax.Precision.HIGHEST
NX, NY, NZ = 4, 4, 8
ROWS, RANK, WIDE = 256, 32, 1792
CH = 256
NCH = WIDE // CH
NN = (((1,), (0,)), ((), ()))
NT = (((1,), (1,)), ((), ()))
TN = (((0,), (0,)), ((), ()))


def split(value):
    high = value.astype(BF16)
    low = (value - high.astype(F32)).astype(BF16)
    return high, low


def product(a, b, dims):
    return lax.dot_general(a, b, dims, preferred_element_type=F32)


def inverse_factor(gram):
    row = lax.broadcasted_iota(jnp.int32, (RANK, RANK), 0)
    lane = lax.broadcasted_iota(jnp.int32, (RANK, RANK), 1)
    unit = jnp.where(row == lane, 1.0, 0.0).astype(F32)
    pivots = jnp.ones((RANK, RANK), F32)
    for j in range(RANK):
        column = jnp.broadcast_to(gram[:, j : j + 1], (RANK, RANK))
        pivot = jnp.broadcast_to(column[j : j + 1, :], (RANK, RANK))
        pivots = jnp.where(row == j, pivot, pivots)
        if j < RANK - 1:
            factor = jnp.where(row > j, column / pivot, 0.0)
            gram = gram - factor * gram[j : j + 1, :]
            unit = unit - factor * unit[j : j + 1, :]
    return unit * lax.rsqrt(pivots)


def main_kernel(
    grad0, grad1, error0, error1, q0, q1,
    sum0, sum1, next0, next1, new0, new1,
    graw, full, qv, fhi, flo, psend, precv, ybuf, zbuf, lmine, left,
    tbuf, xr, zs, zr, tsum, inv, wide,
    ldg, lde, ldq, s1, r1, s2, r2, s3, r3, s4, r4,
    sx, rx, sz, rz, sgz, rgz, sgx, rgx,
):
    grads, errors, qs = (grad0, grad1), (error0, error1), (q0, q1)
    sums, nexts, news = (sum0, sum1), (next0, next1), (new0, new1)
    dp, tensor = lax.axis_index("dp"), lax.axis_index("tensor")
    z, x, y, c = dp // NX, dp % NX, tensor // 2, tensor % 2

    def device(dz=0, dx=0, dy=0, dc=0):
        return (
            lax.rem(z + dz, NZ) * NX + lax.rem(x + dx, NX),
            lax.rem(y + dy, NY) * 2 + lax.rem(c + dc, 2),
        )

    def send(src, dst, send_sem, recv_sem, to):
        pltpu.make_async_remote_copy(
            src_ref=src, dst_ref=dst, send_sem=send_sem, recv_sem=recv_sem,
            device_id=to, device_id_type=MESH,
        ).start()

    def wait(ref, sem):
        pltpu.make_async_copy(ref, ref, sem).wait()

    for b in range(2):
        pltpu.make_async_copy(qs[b], qv.at[b], ldq.at[b]).start()
        for j in range(NCH):
            cols = pl.ds(j * CH, CH)
            pltpu.make_async_copy(errors[b].at[0, :, cols], full.at[b, j], lde.at[b, j]).start()
            pltpu.make_async_copy(grads[b].at[0, :, cols], graw.at[b, j], ldg.at[b, j]).start()

    barrier = pltpu.get_barrier_semaphore()
    xc = [(dx, dc) for dx in (2, 1, 3, 0) for dc in range(2) if (dx, dc) != (0, 0)]
    peers = [device(dx=dx, dc=dc) for dx, dc in xc]
    peers += [device(dy=k) for k in (2, 1, 3)]
    peers += [device(dz=k) for k in (4, 3, 5, 2, 6, 1, 7)]
    for peer in peers:
        pl.semaphore_signal(barrier, inc=1, device_id=peer, device_id_type=MESH)

    for b in range(2):
        wait(qv.at[b], ldq.at[b])
        qhi, qlo = split(qv[b])
        both = jnp.concatenate([qhi, qlo], axis=0)
        acc = jnp.zeros((RANK, ROWS), F32)
        for j in range(NCH):
            wait(full.at[b, j], lde.at[b, j])
            wait(graw.at[b, j], ldg.at[b, j])
            value = graw[b, j].astype(F32) + full[b, j]
            high, low = split(value)
            full[b, j], fhi[b, j], flo[b, j] = value, high, low
            cols = slice(j * CH, (j + 1) * CH)
            first = product(both[:, cols], high, NT)
            acc += first[:RANK] + first[RANK:] + product(qhi[:, cols], low, NT)
        for k in range(4):
            psend[4 * b + k] = acc[8 * k : 8 * k + 8]
        if b == 0:
            pl.semaphore_wait(barrier, len(peers))

    mine = c * NX + x
    for dx, dc in xc:
        there = lax.rem(c + dc, 2) * NX + lax.rem(x + dx, NX)
        send(psend.at[there], precv.at[dc * NX + dx - 1], s1, r1, device(dx=dx, dc=dc))
    wait(precv, r1)
    part = psend[mine]
    for k in range(7):
        part += precv[k]
    ybuf[0] = part
    for k in (2, 1, 3):
        send(ybuf.at[0], ybuf.at[k], s2, r2, device(dy=k))
    wait(ybuf.at[pl.ds(1, 3)], r2)
    part = ybuf[y]
    for k in range(1, NY):
        part += ybuf[lax.rem(y - k + NY, NY)]
    zbuf[0] = part
    for k in (4, 3, 5, 2, 6, 1, 7):
        send(zbuf.at[0], zbuf.at[k], s3, r3, device(dz=k))
    wait(zbuf.at[pl.ds(1, 7)], r3)
    part = zbuf[z]
    for k in range(1, NZ):
        part += zbuf[lax.rem(z - k + NZ, NZ)]
    lmine[...] = part
    for dx, dc in xc:
        send(lmine, left.at[mine], s4, r4.at[c], device(dx=dx, dc=dc))
    pltpu.make_async_copy(lmine, left.at[mine], r4.at[c]).start()

    lefts, lhs = [], []
    for b in range(2):
        wait(left.at[pl.ds(4 * b, 4)], r4.at[b])
        lefts.append(left[4 * b : 4 * b + 4].reshape(RANK, ROWS))
        lhi, llo = split(lefts[b])
        lhs.append((jnp.concatenate([lhi, llo], axis=0), lhi))
    chunks = [lax.rem(z + 3 + k, NCH) for k in range(NCH)]
    for chunk in chunks:
        for b in range(2):
            first = product(lhs[b][0], fhi[b, chunk], NN)
            value = first[:RANK] + first[RANK:] + product(lhs[b][1], flo[b, chunk], NN)
            tbuf[chunk, 2 * b] = value[:16]
            tbuf[chunk, 2 * b + 1] = value[16:]
        for dx in (2, 1, 3):
            send(
                tbuf.at[chunk, lax.rem(x + dx, NX)], xr.at[chunk, dx - 1], sx, rx.at[chunk], device(dx=dx)
            )

    for chunk in chunks:
        wait(xr.at[chunk], rx.at[chunk])
        zs[chunk] = tbuf[chunk, x] + xr[chunk, 0] + xr[chunk, 1] + xr[chunk, 2]

        @pl.when(chunk != z)
        def _():
            send(
                zs.at[chunk], zr.at[lax.rem(chunk - z + NZ, NZ)], sz.at[chunk], rz,
                device(dz=chunk - z + NZ),
            )

    for b in range(2):
        gram = lax.dot_general(lefts[b], lefts[b], NT, precision=HIGHEST, preferred_element_type=F32)
        inverse = inverse_factor(gram)
        ortho = lax.dot_general(inverse, lefts[b], NN, precision=HIGHEST, preferred_element_type=F32)
        weight = lax.dot_general(inverse, ortho, TN, precision=HIGHEST, preferred_element_type=F32)
        whi = weight.astype(BF16).astype(F32)
        wide[b] = jnp.concatenate([whi, whi, weight - whi], axis=0).T.astype(BF16)
        inv[b] = inverse

    @pl.when(z < NCH)
    def _():
        wait(zr.at[pl.ds(1, 7)], rz)
        part = zs[z]
        for k in range(1, NZ):
            part += zr[k]
        tsum[z, x] = part
        for k in (4, 3, 5, 2, 6, 1, 7):
            send(tsum.at[z, x], tsum.at[z, x], sgz, rgz.at[z], device(dz=k))
        for dx in (2, 1, 3):
            send(tsum.at[z, x], tsum.at[z, x], sgx, rgx.at[z, dx - 1], device(dx=dx))

    def triple(value):
        high, low = split(value)
        return jnp.concatenate([high, low, high], axis=0)

    for b in range(2):
        for j in range(NCH):
            own = tbuf[j, 2 * b : 2 * b + 2].reshape(RANK, CH)
            cols = slice(j * CH, (j + 1) * CH)
            news[b][:, cols] = full[b, j] - product(wide[b], triple(own), NN)

    for k in (1, 7, 2, 6, 3, 5, 4):
        at = lax.rem(z + k, NZ)

        @pl.when(at < NCH)
        def _():
            wait(tsum.at[at, x], rgz.at[at])
            for dx in (2, 1, 3):
                send(tsum.at[at, x], tsum.at[at, x], sgx, rgx.at[at, dx - 1], device(dx=dx))

    for k in (0, 1, 7, 2, 6, 3, 5, 4):
        at = lax.rem(z + k, NZ)

        @pl.when(at < NCH)
        def _():
            for dx in (1, 3, 2):
                wait(tsum.at[at, lax.rem(x - dx + NX, NX)], rgx.at[at, dx - 1])
            cols = pl.ds(pl.multiple_of(at * CH, CH), CH)
            for b in range(2):
                total = tsum[at, 2 * b : 2 * b + 2].reshape(RANK, CH)
                sums[b][:, cols] = product(wide[b], triple(total), NN).astype(BF16)
                nexts[b][:, cols] = lax.dot_general(
                    inv[b], total, NN, precision=HIGHEST, preferred_element_type=F32
                )

    wait(precv, s1)
    wait(ybuf.at[pl.ds(1, 3)], s2)
    wait(zbuf.at[pl.ds(1, 7)], s3)
    wait(precv, s4)
    wait(xr, sx)
    wait(xr, sgx)
    for k in range(NCH):

        @pl.when(k != z)
        def _():
            wait(zs.at[k], sz.at[k])

    @pl.when(z < NCH)
    def _():
        wait(zr.at[pl.ds(1, 7)], sgz)


def store_kernel(*refs):
    ins, outs, sem = refs[:6], refs[6:12], refs[12]
    copies = [pltpu.make_async_copy(a, b, sem.at[i]) for i, (a, b) in enumerate(zip(ins, outs))]
    for copy in copies:
        copy.start()
    for copy in copies:
        copy.wait()


def shards(grad0, grad1, error0, error1, q0, q1):
    vmem = pl.BlockSpec(memory_space=pltpu.VMEM)
    hbm = pl.BlockSpec(memory_space=pltpu.HBM)
    shapes = [
        ((ROWS, WIDE), BF16), ((ROWS, WIDE), BF16),
        ((RANK, WIDE), F32), ((RANK, WIDE), F32),
        ((ROWS, WIDE), F32), ((ROWS, WIDE), F32),
    ]
    dma = pltpu.SemaphoreType.DMA
    scratch = [
        pltpu.VMEM((2, NCH, ROWS, CH), BF16),
        pltpu.VMEM((2, NCH, ROWS, CH), F32),
        pltpu.VMEM((2, RANK, WIDE), F32),
        pltpu.VMEM((2, NCH, ROWS, CH), BF16),
        pltpu.VMEM((2, NCH, ROWS, CH), BF16),
        pltpu.VMEM((8, 8, ROWS), F32),
        pltpu.VMEM((7, 8, ROWS), F32),
        pltpu.VMEM((NY, 8, ROWS), F32),
        pltpu.VMEM((NZ, 8, ROWS), F32),
        pltpu.VMEM((8, ROWS), F32),
        pltpu.VMEM((8, 8, ROWS), F32),
        pltpu.VMEM((NCH, NX, 16, CH), F32),
        pltpu.VMEM((NCH, NX - 1, 16, CH), F32),
        pltpu.VMEM((NCH, 16, CH), F32),
        pltpu.VMEM((NZ, 16, CH), F32),
        pltpu.VMEM((NCH, NX, 16, CH), F32),
        pltpu.VMEM((2, RANK, RANK), F32),
        pltpu.VMEM((2, ROWS, 3 * RANK), BF16),
        dma((2, NCH)), dma((2, NCH)), dma((2,)),
        dma, dma, dma, dma, dma, dma, dma, dma((2,)),
        dma, dma((NCH,)), dma((NCH,)), dma,
        dma, dma((NCH,)), dma, dma((NCH, NX - 1)),
    ]
    held = pl.pallas_call(
        main_kernel,
        out_shape=[pltpu.VMEM(s, d) for s, d in shapes],
        in_specs=[hbm] * 6,
        out_specs=[vmem] * 6,
        scratch_shapes=scratch,
        name="compress",
        compiler_params=pltpu.CompilerParams(
            collective_id=0, has_side_effects=True, vmem_limit_bytes=36 << 20
        ),
    )(*[pltpu.with_memory_space_constraint(a, pltpu.HBM) for a in (grad0, grad1, error0, error1, q0.T, q1.T)])
    outs = pl.pallas_call(
        store_kernel,
        out_shape=[jax.ShapeDtypeStruct(s, d) for s, d in shapes],
        in_specs=[vmem] * 6,
        out_specs=[hbm] * 6,
        scratch_shapes=[dma((6,))],
        name="store",
        compiler_params=pltpu.CompilerParams(vmem_limit_bytes=4 << 20),
    )(*held)
    sum0, sum1, next0, next1, new0, new1 = outs
    return sum0, sum1, next0.T, next1.T, new0[None], new1[None]


def solution(mesh):
    wide = P("dp", None, "tensor")
    tall = P("tensor", None)
    flat = P(None, "tensor")
    return jax.shard_map(
        shards,
        mesh=mesh,
        in_specs=(wide, wide, wide, wide, tall, tall),
        out_specs=(flat, flat, tall, tall, wide, wide),
        check_vma=False,
    )
```

time: 418 us -> 55.9 us (0.13)
  waiting for transfers between devices: 360 us -> 0 us
  Pallas kernels: 0 us -> 55.1 us
  matrix products: 27.4 us -> 0 us
  other arithmetic: 13.4 us -> 0 us
  between operations: 13.9 us -> 0.64 us
    psum x3 -> x0, waiting for transfers between devices: 359 us -> none  [the longest x1 150 us: shards(): gate_next, up_next = lax.psum((gate_own, up_own), 'dp')]
    pallas_call x0 -> x2, Pallas kernels: none -> 55.1 us  [the longest x1 52.4 us: shards(): pl.pallas_call(main_kernel, out_shape=[pltpu.VMEM(s, d) for s, d in shape...]
    dot_general x10 -> x0, matrix products: 25.4 us -> none  [the longest x1 4.07 us: shards(): gate_part = jnp.dot(gate_full, gate_q, precision=lax.Precision.HIGHEST)]
    another operation x10 -> x0, other arithmetic: 13.4 us -> none  [the longest x6 7.19 us: orthogonal(): factor = jnp.linalg.cholesky(gram)]
  transfers between devices with their start and end apart: 3 -> 0, of which waited for: 3 -> 0; matrix products, arithmetic and copies ran while one was open for 0% -> 0% of each run, Pallas kernels for 0% -> 0%
where the time goes in v1:
time: 55.9 us; the launch traced here: 55.7 us
  Pallas kernels  55.1 us (99%)
  between operations  0.64 us (1%)
    pallas_call x1, Pallas kernels, shards(): pl.pallas_call(main_kernel, out_shape=[pltpu.VMEM(s, d) for s, d in shape...  52.4 us
    pallas_call x1, Pallas kernels, shards(): pl.pallas_call(store_kernel, out_shape=[jax.ShapeDtypeStruct(s, d) for s,...  2.64 us

profile of v1, /device:TPU:8, one launch (start us, length us, event | category | flops | bytes accessed | tf_op | source)
XLA Modules:
  0.0 55.7 jit_solution(6144051426564729986)
XLA Ops:
  0.6 52.4 %compress.1 = (bf16[256,1792]{1,0:T(8,128)(2,1)S(1)}, bf16[256,1792]{1,0:T(8,128)(2,1)S(1)}, f32[32,1792]{1,0:T(8,128)S(1)}, f32[32,1792]{1,0:T(8,128)S(1)}, f32...) custom-call(bf16[1,256,1792]{2,1,0:T(8,128)(2,1)} %grad0.1, bf16[1,256,1792]{2,1,0:T(8,128)(2,1)} %grad1.1, ...), custom_call_target="tpu_custom_call" | custom-call | tf_op jit(solution)/shard_map/compress/pallas_call | solution.py:280
  53.1 2.6 %store.1 = (bf16[256,1792]{1,0:T(8,128)(2,1)}, bf16[256,1792]{1,0:T(8,128)(2,1)}, f32[32,1792]{1,0:T(8,128)}, f32[32,1792]{1,0:T(8,128)}, f32[256,1792]{1,0:T(8,128)}, /*index=5*/f32[256,1792]{1,0:T(8,128)}) custom-call(bf16[256,1792]{1,0:T(8,128)(2,1)S(1)} %get-tuple-element.18.refs_0_, bf16[256,1792]{1,0:T(8,128)(2,1)S(1)} %get-tuple-element.19.refs_1_, ...), custom_call_target="tpu_custom_call" | custom-call | tf_op jit(solution)/shard_map/store/pallas_call | solution.py:291

commit v2 on v1

v2 whole, which is shorter than its diff:
```python
import functools

import jax
import jax.numpy as jnp
from jax import lax
from jax.experimental import pallas as pl
from jax.experimental.pallas import tpu as pltpu
from jax.sharding import PartitionSpec as P

MESH = pl.DeviceIdType.MESH
F32, BF16 = jnp.float32, jnp.bfloat16
HIGHEST = lax.Precision.HIGHEST
NX, NY, NZ = 4, 4, 8
ROWS, RANK, WIDE = 256, 32, 1792
CH = 256
NCH = WIDE // CH
NN = (((1,), (0,)), ((), ()))
NT = (((1,), (1,)), ((), ()))
TN = (((0,), (0,)), ((), ()))


def split(value):
    high = value.astype(BF16)
    low = (value - high.astype(F32)).astype(BF16)
    return high, low


def product(a, b, dims):
    return lax.dot_general(a, b, dims, preferred_element_type=F32)


def triple(value):
    high, low = split(value)
    return jnp.concatenate([high, low, high], axis=0)


def inverse_factors(gram0, gram1):
    row = lax.broadcasted_iota(jnp.int32, (8, 128), 0)
    lane = lax.broadcasted_iota(jnp.int32, (8, 128), 1)
    first = lane < 64

    def spread(value, shape=(8, 128)):
        return jnp.broadcast_to(value, shape)

    def column(i, j):
        rows = slice(8 * i, 8 * i + 8)
        return jnp.where(first, spread(gram0[rows, j : j + 1]), spread(gram1[rows, j : j + 1]))

    parts = RANK // 8
    columns = [[column(i, j) if i >= j // 8 else None for i in range(parts)] for j in range(RANK)]
    unit = [jnp.where((lane == row + 8 * i) | (lane == row + 8 * i + 64), 1.0, 0.0) for i in range(parts)]
    pivots = [jnp.ones((8, 128), F32) for _ in range(parts)]
    for j in range(RANK):
        at, sub = j // 8, j % 8
        now = columns[j]
        pivot = spread(now[at][sub : sub + 1])
        pivots[at] = jnp.where(row == sub, pivot, pivots[at])
        if j == RANK - 1:
            break
        scale = 1.0 / pivot
        factor = [now[i] * scale if i >= at else None for i in range(parts)]
        factor[at] = jnp.where(row > sub, factor[at], 0.0)
        for k in range(j + 1, RANK):
            entry = spread(now[k // 8][k % 8 : k % 8 + 1])
            for i in range(k // 8, parts):
                columns[k][i] = columns[k][i] - factor[i] * entry
        entry = spread(unit[at][sub : sub + 1])
        for i in range(at, parts):
            unit[i] = unit[i] - factor[i] * entry
    both = jnp.concatenate([unit[i] * lax.rsqrt(pivots[i]) for i in range(parts)], axis=0)
    return both[:, :RANK], both[:, 64 : 64 + RANK]


def main_kernel(
    grad0, grad1, error0, error1, q0, q1,
    sum0, sum1, next0, next1, new0, new1,
    graw, full, qv, fhi, flo, psend, precv, cbuf, zbuf, lmine, left,
    tbuf, xr, zs, zr, tsum, wide,
    ldg, lde, ldq, s1, r1, s2, r2, s3, r3, s4, r4,
    sx, rx, sz, rz, sgz, rgz, sgx, rgx,
):
    grads, errors, qs = (grad0, grad1), (error0, error1), (q0, q1)
    sums, nexts, news = (sum0, sum1), (next0, next1), (new0, new1)
    dp, tensor = lax.axis_index("dp"), lax.axis_index("tensor")
    z, x = lax.div(dp, NX), lax.rem(dp, NX)
    y, c = lax.div(tensor, 2), lax.rem(tensor, 2)

    def device(dz=0, dx=0, dy=0, dc=0):
        return (
            lax.rem(z + dz, NZ) * NX + lax.rem(x + dx, NX),
            lax.rem(y + dy, NY) * 2 + lax.rem(c + dc, 2),
        )

    def send(src, dst, send_sem, recv_sem, to):
        pltpu.make_async_remote_copy(
            src_ref=src, dst_ref=dst, send_sem=send_sem, recv_sem=recv_sem,
            device_id=to, device_id_type=MESH,
        ).start()

    def wait(ref, sem):
        pltpu.make_async_copy(ref, ref, sem).wait()

    groups = [(0, 0, 4), (0, 4, 7), (1, 0, 4), (1, 4, 7)]

    def load(number):
        b, low, high = groups[number]
        cols = pl.ds(low * CH, (high - low) * CH)
        pltpu.make_async_copy(errors[b].at[0, :, cols], full.at[b, :, cols], lde.at[number]).start()
        pltpu.make_async_copy(grads[b].at[0, :, cols], graw.at[b, :, cols], ldg.at[number]).start()

    pltpu.make_async_copy(qs[0], qv.at[0], ldq.at[0]).start()
    for number in range(3):
        load(number)
    pltpu.make_async_copy(qs[1], qv.at[1], ldq.at[1]).start()

    barrier = pltpu.get_barrier_semaphore()
    plane = [(dx, dy) for dx in range(NX) for dy in range(NY) if (dx, dy) != (0, 0)]
    plane.sort(key=lambda d: -(min(d[0], NX - d[0]) + min(d[1], NY - d[1])))
    column = (4, 3, 5, 2, 6, 1, 7)
    peers = [device(dx=dx, dy=dy) for dx, dy in plane]
    peers += [device(dc=1)] + [device(dz=k) for k in column]
    for peer in peers:
        pl.semaphore_signal(barrier, inc=1, device_id=peer, device_id_type=MESH)

    for number, (b, low, high) in enumerate(groups):
        if low == 0:
            wait(qv.at[b], ldq.at[b])
            qhi, qlo = split(qv[b])
            both = jnp.concatenate([qhi, qlo], axis=0)
            acc = jnp.zeros((RANK, ROWS), F32)
        cols = pl.ds(low * CH, (high - low) * CH)
        wait(full.at[b, :, cols], lde.at[number])
        wait(graw.at[b, :, cols], ldg.at[number])
        if number + 3 < len(groups):
            load(number + 3)
        for j in range(low, high):
            cols = slice(j * CH, (j + 1) * CH)
            value = graw[b, :, cols].astype(F32) + full[b, :, cols]
            top, rest = split(value)
            full[b, :, cols], fhi[b, :, cols], flo[b, :, cols] = value, top, rest
            first = product(both[:, cols], top, NT)
            acc += first[:RANK] + first[RANK:] + product(qhi[:, cols], rest, NT)
        if high == NCH:
            for k in range(8):
                psend[8 * b + k] = acc[8 * (k // 2) : 8 * (k // 2) + 8, 128 * (k % 2) : 128 * (k % 2) + 128]
    pl.semaphore_wait(barrier, len(peers))

    mine = x * NY + y
    for dx, dy in plane:
        there = lax.rem(x + dx, NX) * NY + lax.rem(y + dy, NY)
        send(psend.at[there], precv.at[dx * NY + dy - 1], s1, r1, device(dx=dx, dy=dy))
    wait(precv, r1)
    part = psend[mine]
    for k in range(15):
        part += precv[k]
    cbuf[0] = part
    send(cbuf.at[0], cbuf.at[1], s2, r2, device(dc=1))
    wait(cbuf.at[1], r2)
    zbuf[0] = cbuf[0] + cbuf[1]
    for k in column:
        send(zbuf.at[0], zbuf.at[k], s3, r3, device(dz=k))
    wait(zbuf.at[pl.ds(1, 7)], r3)
    part = zbuf[z]
    for k in range(1, NZ):
        part += zbuf[lax.rem(z - k + NZ, NZ)]
    lmine[...] = part
    for dx, dy in plane:
        send(lmine, left.at[mine], s4, r4.at[lax.div(x, 2)], device(dx=dx, dy=dy))
    pltpu.make_async_copy(lmine, left.at[mine], r4.at[lax.div(x, 2)]).start()

    lefts, lhs = [], []
    for b in range(2):
        wait(left.at[pl.ds(8 * b, 8)], r4.at[b])
        rows = [jnp.concatenate([left[8 * b + 2 * k], left[8 * b + 2 * k + 1]], axis=1) for k in range(4)]
        lefts.append(jnp.concatenate(rows, axis=0))
        lhi, llo = split(lefts[b])
        lhs.append((jnp.concatenate([lhi, llo], axis=0), lhi))

    skip = NZ - 1 - z
    skip = lax.div(skip, 4) * 2 * (skip - 4) + (1 - lax.div(skip, 4)) * (7 - 2 * skip)
    order = []
    for k in range(NCH):
        i = k + lax.div(k - skip + NZ, NZ)
        order.append(lax.rem(z + 4 + (1 - 2 * lax.rem(i, 2)) * lax.div(i + 1, 2), NZ))

    def columns(chunk):
        return pl.ds(pl.multiple_of(chunk * CH, CH), CH)

    for chunk in order:
        for b in range(2):
            cols = columns(chunk)
            first = product(lhs[b][0], fhi[b, :, cols], NN)
            value = first[:RANK] + first[RANK:] + product(lhs[b][1], flo[b, :, cols], NN)
            tbuf[chunk, 2 * b] = value[:16]
            tbuf[chunk, 2 * b + 1] = value[16:]
        for dx in (2, 1, 3):
            send(
                tbuf.at[chunk, lax.rem(x + dx, NX)], xr.at[chunk, dx - 1], sx, rx.at[chunk], device(dx=dx)
            )

    for k, chunk in enumerate(order):
        wait(xr.at[chunk], rx.at[chunk])
        zs[chunk] = tbuf[chunk, x] + xr[chunk, 0] + xr[chunk, 1] + xr[chunk, 2]

        def pass_on(k=k, chunk=chunk):
            away = lax.rem(chunk - z + NZ, NZ)
            send(zs.at[chunk], zr.at[away], sz.at[k], rz, device(dz=away))

        if k < NCH - 1:
            pass_on()
        else:
            pl.when(z == NZ - 1)(pass_on)

    grams = [
        lax.dot_general(a, a, NT, precision=HIGHEST, preferred_element_type=F32) for a in lefts
    ]
    inverses = inverse_factors(*grams)
    for b in range(2):
        ortho = lax.dot_general(inverses[b], lefts[b], NN, precision=HIGHEST, preferred_element_type=F32)
        weight = lax.dot_general(inverses[b], ortho, TN, precision=HIGHEST, preferred_element_type=F32)
        weight = jnp.concatenate([weight, inverses[b].T], axis=1)
        top = weight.astype(BF16).astype(F32)
        wide[b] = jnp.concatenate([top, top, weight - top], axis=0).T.astype(BF16)

    @pl.when(z < NCH)
    def _():
        wait(zr.at[pl.ds(1, 7)], rz)
        part = zs[z]
        for k in range(1, NZ):
            part += zr[k]
        tsum[z, x] = part
        for k in column:
            send(tsum.at[z, x], tsum.at[z, x], sgz, rgz.at[z], device(dz=k))
        for dx in (2, 1, 3):
            send(tsum.at[z, x], tsum.at[z, x], sgx, rgx.at[z, dx - 1], device(dx=dx))

    for b in range(2):
        for j in range(NCH):
            own = tbuf[j, 2 * b : 2 * b + 2].reshape(RANK, CH)
            cols = slice(j * CH, (j + 1) * CH)
            news[b][:, cols] = full[b, :, cols] - product(wide[b, :ROWS], triple(own), NN)

    for k in reversed(range(NCH)):

        def forward(chunk=order[k]):
            wait(tsum.at[chunk, x], rgz.at[chunk])
            for dx in (2, 1, 3):
                send(tsum.at[chunk, x], tsum.at[chunk, x], sgx, rgx.at[chunk, dx - 1], device(dx=dx))

        if k < NCH - 1:
            forward()
        else:
            pl.when(z == NZ - 1)(forward)

    for chunk in reversed(order):
        for dx in (1, 3, 2):
            wait(tsum.at[chunk, lax.rem(x - dx + NX, NX)], rgx.at[chunk, dx - 1])
        cols = columns(chunk)
        for b in range(2):
            total = tsum[chunk, 2 * b : 2 * b + 2].reshape(RANK, CH)
            value = product(wide[b], triple(total), NN)
            sums[b][:, cols] = value[:ROWS].astype(BF16)
            nexts[b][:, cols] = value[ROWS:]

    wait(precv, s1)
    wait(cbuf.at[1], s2)
    wait(zbuf.at[pl.ds(1, 7)], s3)
    wait(precv, s4)
    wait(xr, sx)
    wait(xr, sgx)
    for k in range(NCH - 1):
        wait(zs.at[k], sz.at[k])

    @pl.when(z == NZ - 1)
    def _():
        wait(zs.at[0], sz.at[NCH - 1])

    @pl.when(z < NCH)
    def _():
        wait(zr.at[pl.ds(1, 7)], sgz)


def store_kernel(*refs):
    ins, outs, sem = refs[:6], refs[6:12], refs[12]
    copies = [pltpu.make_async_copy(a, b, sem.at[i]) for i, (a, b) in enumerate(zip(ins, outs))]
    for copy in copies:
        copy.start()
    for copy in copies:
        copy.wait()


def shards(grad0, grad1, error0, error1, q0, q1):
    args = (grad0, grad1, error0, error1, q0.T, q1.T)
    vmem = pl.BlockSpec(memory_space=pltpu.VMEM)
    hbm = pl.BlockSpec(memory_space=pltpu.HBM)
    shapes = [
        ((ROWS, WIDE), BF16), ((ROWS, WIDE), BF16),
        ((RANK, WIDE), F32), ((RANK, WIDE), F32),
        ((ROWS, WIDE), F32), ((ROWS, WIDE), F32),
    ]
    dma = pltpu.SemaphoreType.DMA
    scratch = [
        pltpu.VMEM((2, ROWS, WIDE), BF16),
        pltpu.VMEM((2, ROWS, WIDE), F32),
        pltpu.VMEM((2, RANK, WIDE), F32),
        pltpu.VMEM((2, ROWS, WIDE), BF16),
        pltpu.VMEM((2, ROWS, WIDE), BF16),
        pltpu.VMEM((16, 8, 128), F32),
        pltpu.VMEM((15, 8, 128), F32),
        pltpu.VMEM((2, 8, 128), F32),
        pltpu.VMEM((NZ, 8, 128), F32),
        pltpu.VMEM((8, 128), F32),
        pltpu.VMEM((16, 8, 128), F32),
        pltpu.VMEM((NCH, NX, 16, CH), F32),
        pltpu.VMEM((NCH, NX - 1, 16, CH), F32),
        pltpu.VMEM((NCH, 16, CH), F32),
        pltpu.VMEM((NZ, 16, CH), F32),
        pltpu.VMEM((NCH, NX, 16, CH), F32),
        pltpu.VMEM((2, ROWS + RANK, 3 * RANK), BF16),
        dma((4,)), dma((4,)), dma((2,)),
        dma, dma, dma, dma, dma, dma, dma, dma((2,)),
        dma, dma((NCH,)), dma((NCH,)), dma,
        dma, dma((NCH,)), dma, dma((NCH, NX - 1)),
    ]
    held = pl.pallas_call(
        main_kernel,
        out_shape=[pltpu.VMEM(s, d) for s, d in shapes],
        in_specs=[hbm] * 6,
        out_specs=[vmem] * 6,
        scratch_shapes=scratch,
        name="compress",
        compiler_params=pltpu.CompilerParams(
            collective_id=0, has_side_effects=True, vmem_limit_bytes=36 << 20
        ),
    )(*[pltpu.with_memory_space_constraint(a, pltpu.HBM) for a in args])
    outs = pl.pallas_call(
        store_kernel,
        out_shape=[jax.ShapeDtypeStruct(s, d) for s, d in shapes],
        in_specs=[vmem] * 6,
        out_specs=[hbm] * 6,
        scratch_shapes=[dma((6,))],
        name="store",
        compiler_params=pltpu.CompilerParams(vmem_limit_bytes=4 << 20),
    )(*held)
    sum0, sum1, next0, next1, new0, new1 = outs
    return sum0, sum1, next0.T, next1.T, new0[None], new1[None]


def solution(mesh):
    wide = P("dp", None, "tensor")
    tall = P("tensor", None)
    flat = P(None, "tensor")
    return jax.shard_map(
        shards,
        mesh=mesh,
        in_specs=(wide, wide, wide, wide, tall, tall),
        out_specs=(flat, flat, tall, tall, wide, wide),
        check_vma=False,
    )
```

time: 55.9 us -> 47.2 us (0.84)
  Pallas kernels: 55.1 us -> 46.3 us
    pallas_call x1, Pallas kernels: 52.4 us -> 43.7 us  [shards(): pl.pallas_call(main_kernel, out_shape=[pltpu.VMEM(s, d) for s, d in shape...]
where the time goes in v2:
time: 47.2 us; the launch traced here: 46.9 us
  Pallas kernels  46.3 us (98%)
  between operations  0.64 us (1%)
    pallas_call x1, Pallas kernels, shards(): pl.pallas_call(main_kernel, out_shape=[pltpu.VMEM(s, d) for s, d in shape...  43.7 us
    pallas_call x1, Pallas kernels, shards(): pl.pallas_call(store_kernel, out_shape=[jax.ShapeDtypeStruct(s, d) for s,...  2.64 us

profile of v2, /device:TPU:8, one launch (start us, length us, event | category | flops | bytes accessed | tf_op | source)
XLA Modules:
  0.0 46.9 jit_solution(4338507919608400845)
XLA Ops:
  0.6 43.7 %compress.1 = (bf16[256,1792]{1,0:T(8,128)(2,1)S(1)}, bf16[256,1792]{1,0:T(8,128)(2,1)S(1)}, f32[32,1792]{1,0:T(8,128)S(1)}, f32[32,1792]{1,0:T(8,128)S(1)}, f32...) custom-call(bf16[1,256,1792]{2,1,0:T(8,128)(2,1)} %grad0.1, bf16[1,256,1792]{2,1,0:T(8,128)(2,1)} %grad1.1, ...), custom_call_target="tpu_custom_call" | custom-call | tf_op jit(solution)/shard_map/compress/pallas_call | solution.py:325
  44.3 2.6 %store.1 = (bf16[256,1792]{1,0:T(8,128)(2,1)}, bf16[256,1792]{1,0:T(8,128)(2,1)}, f32[32,1792]{1,0:T(8,128)}, f32[32,1792]{1,0:T(8,128)}, f32[256,1792]{1,0:T(8,128)}, /*index=5*/f32[256,1792]{1,0:T(8,128)}) custom-call(bf16[256,1792]{1,0:T(8,128)(2,1)S(1)} %get-tuple-element.18.refs_0_, bf16[256,1792]{1,0:T(8,128)(2,1)S(1)} %get-tuple-element.19.refs_1_, ...), custom_call_target="tpu_custom_call" | custom-call | tf_op jit(solution)/shard_map/store/pallas_call | solution.py:336

commit v3 on v2

--- a/solution.py
+++ b/solution.py
@@ -14,6 +14,7 @@
 ROWS, RANK, WIDE = 256, 32, 1792
 CH = 256
 NCH = WIDE // CH
+BARE = 4
 NN = (((1,), (0,)), ((), ()))
 NT = (((1,), (1,)), ((), ()))
 TN = (((0,), (0,)), ((), ()))
@@ -73,14 +74,14 @@
 
 def main_kernel(
     grad0, grad1, error0, error1, q0, q1,
-    sum0, sum1, next0, next1, new0, new1,
+    tsum, wide, new0, new1,
     graw, full, qv, fhi, flo, psend, precv, cbuf, zbuf, lmine, left,
-    tbuf, xr, zs, zr, tsum, wide,
+    tbuf, xr, zs, zr,
     ldg, lde, ldq, s1, r1, s2, r2, s3, r3, s4, r4,
     sx, rx, sz, rz, sgz, rgz, sgx, rgx,
 ):
     grads, errors, qs = (grad0, grad1), (error0, error1), (q0, q1)
-    sums, nexts, news = (sum0, sum1), (next0, next1), (new0, new1)
+    news = (new0, new1)
     dp, tensor = lax.axis_index("dp"), lax.axis_index("tensor")
     z, x = lax.div(dp, NX), lax.rem(dp, NX)
     y, c = lax.div(tensor, 2), lax.rem(tensor, 2)
@@ -140,15 +141,27 @@
             full[b, :, cols], fhi[b, :, cols], flo[b, :, cols] = value, top, rest
             first = product(both[:, cols], top, NT)
             acc += first[:RANK] + first[RANK:] + product(qhi[:, cols], rest, NT)
-        if high == NCH:
-            for k in range(8):
-                psend[8 * b + k] = acc[8 * (k // 2) : 8 * (k // 2) + 8, 128 * (k % 2) : 128 * (k % 2) + 128]
-    pl.semaphore_wait(barrier, len(peers))
+        if high < NCH:
+            continue
+        for k in range(8):
+            psend[8 * b + k] = acc[8 * (k // 2) : 8 * (k // 2) + 8, 128 * (k % 2) : 128 * (k % 2) + 128]
+        if b == 0:
+            pl.semaphore_wait(barrier, len(peers))
+        for xo in (2 * b, 2 * b + 1):
+            for dy in (2, 1, 3, 0):
+
+                def give(xo=xo, dy=dy):
+                    yo = lax.rem(y + dy, NY)
+                    slot = lax.rem(xo - x + NX, NX) * NY + dy - 1
+                    to = (z * NX + xo, yo * 2 + c)
+                    send(psend.at[xo * NY + yo], precv.at[slot], s1, r1, to)
+
+                if dy:
+                    give()
+                else:
+                    pl.when(x != xo)(give)
 
     mine = x * NY + y
-    for dx, dy in plane:
-        there = lax.rem(x + dx, NX) * NY + lax.rem(y + dy, NY)
-        send(psend.at[there], precv.at[dx * NY + dy - 1], s1, r1, device(dx=dx, dy=dy))
     wait(precv, r1)
     part = psend[mine]
     for k in range(15):
@@ -168,48 +181,43 @@
         send(lmine, left.at[mine], s4, r4.at[lax.div(x, 2)], device(dx=dx, dy=dy))
     pltpu.make_async_copy(lmine, left.at[mine], r4.at[lax.div(x, 2)]).start()
 
-    lefts, lhs = [], []
+    skip = lax.rem(BARE - z + NZ, NZ)
+    skip = lax.div(skip, 4) * 2 * (skip - 4) + (1 - lax.div(skip, 4)) * (7 - 2 * skip)
+    order = []
+    for k in range(NCH):
+        i = k + lax.div(k - skip + NZ, NZ)
+        away = lax.rem(4 + (1 - 2 * lax.rem(i, 2)) * lax.div(i + 1, 2), NZ)
+        order.append((lax.rem(z + away + NZ - 1 - BARE, NZ), away))
+    owned = lax.rem(z + NZ - 1 - BARE, NZ)
+
+    lefts = []
     for b in range(2):
         wait(left.at[pl.ds(8 * b, 8)], r4.at[b])
         rows = [jnp.concatenate([left[8 * b + 2 * k], left[8 * b + 2 * k + 1]], axis=1) for k in range(4)]
         lefts.append(jnp.concatenate(rows, axis=0))
         lhi, llo = split(lefts[b])
-        lhs.append((jnp.concatenate([lhi, llo], axis=0), lhi))
-
-    skip = NZ - 1 - z
-    skip = lax.div(skip, 4) * 2 * (skip - 4) + (1 - lax.div(skip, 4)) * (7 - 2 * skip)
-    order = []
-    for k in range(NCH):
-        i = k + lax.div(k - skip + NZ, NZ)
-        order.append(lax.rem(z + 4 + (1 - 2 * lax.rem(i, 2)) * lax.div(i + 1, 2), NZ))
-
-    def columns(chunk):
-        return pl.ds(pl.multiple_of(chunk * CH, CH), CH)
-
-    for chunk in order:
-        for b in range(2):
-            cols = columns(chunk)
-            first = product(lhs[b][0], fhi[b, :, cols], NN)
-            value = first[:RANK] + first[RANK:] + product(lhs[b][1], flo[b, :, cols], NN)
-            tbuf[chunk, 2 * b] = value[:16]
-            tbuf[chunk, 2 * b + 1] = value[16:]
-        for dx in (2, 1, 3):
-            send(
-                tbuf.at[chunk, lax.rem(x + dx, NX)], xr.at[chunk, dx - 1], sx, rx.at[chunk], device(dx=dx)
-            )
-
-    for k, chunk in enumerate(order):
-        wait(xr.at[chunk], rx.at[chunk])
-        zs[chunk] = tbuf[chunk, x] + xr[chunk, 0] + xr[chunk, 1] + xr[chunk, 2]
-
-        def pass_on(k=k, chunk=chunk):
-            away = lax.rem(chunk - z + NZ, NZ)
-            send(zs.at[chunk], zr.at[away], sz.at[k], rz, device(dz=away))
-
-        if k < NCH - 1:
-            pass_on()
-        else:
-            pl.when(z == NZ - 1)(pass_on)
+        both = jnp.concatenate([lhi, llo], axis=0)
+        for chunk, _ in order:
+            cols = pl.ds(pl.multiple_of(chunk * CH, CH), CH)
+            first = product(both, fhi[b, :, cols], NN)
+            value = first[:RANK] + first[RANK:] + product(lhi, flo[b, :, cols], NN)
+            tbuf[chunk, b] = value.reshape(NX, 8, CH)
+            for dx in (2, 1, 3):
+                src = tbuf.at[chunk, b, lax.rem(x + dx, NX)]
+                send(src, xr.at[chunk, b, dx - 1], sx, rx.at[b, chunk], device(dx=dx))
+
+    for b in range(2):
+        for k, (chunk, away) in enumerate(order):
+            wait(xr.at[chunk, b], rx.at[b, chunk])
+            zs[b, chunk] = tbuf[chunk, b, x] + xr[chunk, b, 0] + xr[chunk, b, 1] + xr[chunk, b, 2]
+
+            def pass_on(b=b, k=k, chunk=chunk, away=away):
+                send(zs.at[b, chunk], zr.at[b, away], sz.at[b, k], rz.at[b], device(dz=away))
+
+            if k < NCH - 1:
+                pass_on()
+            else:
+                pl.when(z == BARE)(pass_on)
 
     grams = [
         lax.dot_general(a, a, NT, precision=HIGHEST, preferred_element_type=F32) for a in lefts
@@ -222,45 +230,42 @@
         top = weight.astype(BF16).astype(F32)
         wide[b] = jnp.concatenate([top, top, weight - top], axis=0).T.astype(BF16)
 
-    @pl.when(z < NCH)
-    def _():
-        wait(zr.at[pl.ds(1, 7)], rz)
-        part = zs[z]
-        for k in range(1, NZ):
-            part += zr[k]
-        tsum[z, x] = part
-        for k in column:
-            send(tsum.at[z, x], tsum.at[z, x], sgz, rgz.at[z], device(dz=k))
-        for dx in (2, 1, 3):
-            send(tsum.at[z, x], tsum.at[z, x], sgx, rgx.at[z, dx - 1], device(dx=dx))
+    for b in range(2):
+
+        @pl.when(z != BARE)
+        def _():
+            wait(zr.at[b, pl.ds(1, 7)], rz.at[b])
+            part = zs[b, owned]
+            for k in range(1, NZ):
+                part += zr[b, k]
+            tsum[owned, b, x] = part
+            here = tsum.at[owned, b, x]
+            for k in column:
+                send(here, here, sgz.at[b], rgz.at[b, owned], device(dz=k))
+            for dx in (2, 1, 3):
+                send(here, here, sgx, rgx, device(dx=dx))
 
     for b in range(2):
         for j in range(NCH):
-            own = tbuf[j, 2 * b : 2 * b + 2].reshape(RANK, CH)
+            own = tbuf[j, b].reshape(RANK, CH)
             cols = slice(j * CH, (j + 1) * CH)
             news[b][:, cols] = full[b, :, cols] - product(wide[b, :ROWS], triple(own), NN)
 
-    for k in reversed(range(NCH)):
-
-        def forward(chunk=order[k]):
-            wait(tsum.at[chunk, x], rgz.at[chunk])
-            for dx in (2, 1, 3):
-                send(tsum.at[chunk, x], tsum.at[chunk, x], sgx, rgx.at[chunk, dx - 1], device(dx=dx))
-
-        if k < NCH - 1:
-            forward()
-        else:
-            pl.when(z == NZ - 1)(forward)
-
-    for chunk in reversed(order):
-        for dx in (1, 3, 2):
-            wait(tsum.at[chunk, lax.rem(x - dx + NX, NX)], rgx.at[chunk, dx - 1])
-        cols = columns(chunk)
-        for b in range(2):
-            total = tsum[chunk, 2 * b : 2 * b + 2].reshape(RANK, CH)
-            value = product(wide[b], triple(total), NN)
-            sums[b][:, cols] = value[:ROWS].astype(BF16)
-            nexts[b][:, cols] = value[ROWS:]
+    for b in range(2):
+        for k in reversed(range(NCH)):
+
+            def forward(b=b, chunk=order[k][0]):
+                here = tsum.at[chunk, b, x]
+                wait(here, rgz.at[b, chunk])
+                for dx in (2, 1, 3):
+                    send(here, here, sgx, rgx, device(dx=dx))
+
+            if k < NCH - 1:
+                forward()
+            else:
+                pl.when(z == BARE)(forward)
+
+    wait(xr, rgx)
 
     wait(precv, s1)
     wait(cbuf.at[1], s2)
@@ -268,23 +273,37 @@
     wait(precv, s4)
     wait(xr, sx)
     wait(xr, sgx)
-    for k in range(NCH - 1):
-        wait(zs.at[k], sz.at[k])
-
-    @pl.when(z == NZ - 1)
-    def _():
-        wait(zs.at[0], sz.at[NCH - 1])
-
-    @pl.when(z < NCH)
-    def _():
-        wait(zr.at[pl.ds(1, 7)], sgz)
-
-
-def store_kernel(*refs):
-    ins, outs, sem = refs[:6], refs[6:12], refs[12]
-    copies = [pltpu.make_async_copy(a, b, sem.at[i]) for i, (a, b) in enumerate(zip(ins, outs))]
+    for b in range(2):
+        for k in range(NCH - 1):
+            wait(zs.at[b, k], sz.at[b, k])
+
+        @pl.when(z == BARE)
+        def _():
+            wait(zs.at[b, 0], sz.at[b, NCH - 1])
+
+        @pl.when(z != BARE)
+        def _():
+            wait(zr.at[b, pl.ds(1, 7)], sgz.at[b])
+
+
+def finish_kernel(
+    tsum, wide, new0, new1, sum0, sum1, next0, next1, out0, out1, sums, nexts, sem
+):
+    copies = [pltpu.make_async_copy(new0, out0, sem.at[0]), pltpu.make_async_copy(new1, out1, sem.at[1])]
     for copy in copies:
         copy.start()
+    for low, high in ((0, 4), (4, 7)):
+        for b in range(2):
+            for j in range(low, high):
+                cols = slice(j * CH, (j + 1) * CH)
+                value = product(wide[b], triple(tsum[j, b].reshape(RANK, CH)), NN)
+                sums[b, :, cols] = value[:ROWS].astype(BF16)
+                nexts[b, :, cols] = value[ROWS:]
+            cols = pl.ds(low * CH, (high - low) * CH)
+            for held, out in ((sums, (sum0, sum1)), (nexts, (next0, next1))):
+                copy = pltpu.make_async_copy(held.at[b, :, cols], out[b].at[:, cols], sem.at[len(copies)])
+                copy.start()
+                copies.append(copy)
     for copy in copies:
         copy.wait()
 
@@ -293,11 +312,6 @@
     args = (grad0, grad1, error0, error1, q0.T, q1.T)
     vmem = pl.BlockSpec(memory_space=pltpu.VMEM)
     hbm = pl.BlockSpec(memory_space=pltpu.HBM)
-    shapes = [
-        ((ROWS, WIDE), BF16), ((ROWS, WIDE), BF16),
-        ((RANK, WIDE), F32), ((RANK, WIDE), F32),
-        ((ROWS, WIDE), F32), ((ROWS, WIDE), F32),
-    ]
     dma = pltpu.SemaphoreType.DMA
     scratch = [
         pltpu.VMEM((2, ROWS, WIDE), BF16),
@@ -311,38 +325,51 @@
         pltpu.VMEM((NZ, 8, 128), F32),
         pltpu.VMEM((8, 128), F32),
         pltpu.VMEM((16, 8, 128), F32),
-        pltpu.VMEM((NCH, NX, 16, CH), F32),
-        pltpu.VMEM((NCH, NX - 1, 16, CH), F32),
-        pltpu.VMEM((NCH, 16, CH), F32),
-        pltpu.VMEM((NZ, 16, CH), F32),
-        pltpu.VMEM((NCH, NX, 16, CH), F32),
-        pltpu.VMEM((2, ROWS + RANK, 3 * RANK), BF16),
+        pltpu.VMEM((NCH, 2, NX, 8, CH), F32),
+        pltpu.VMEM((NCH, 2, NX - 1, 8, CH), F32),
+        pltpu.VMEM((2, NCH, 8, CH), F32),
+        pltpu.VMEM((2, NZ, 8, CH), F32),
         dma((4,)), dma((4,)), dma((2,)),
         dma, dma, dma, dma, dma, dma, dma, dma((2,)),
-        dma, dma((NCH,)), dma((NCH,)), dma,
-        dma, dma((NCH,)), dma, dma((NCH, NX - 1)),
+        dma, dma((2, NCH)), dma((2, NCH)), dma((2,)),
+        dma((2,)), dma((2, NCH)), dma, dma,
     ]
     held = pl.pallas_call(
         main_kernel,
-        out_shape=[pltpu.VMEM(s, d) for s, d in shapes],
+        out_shape=[
+            pltpu.VMEM((NCH, 2, NX, 8, CH), F32),
+            pltpu.VMEM((2, ROWS + RANK, 3 * RANK), BF16),
+            pltpu.VMEM((ROWS, WIDE), F32),
+            pltpu.VMEM((ROWS, WIDE), F32),
+        ],
         in_specs=[hbm] * 6,
-        out_specs=[vmem] * 6,
+        out_specs=[vmem] * 4,
         scratch_shapes=scratch,
         name="compress",
         compiler_params=pltpu.CompilerParams(
             collective_id=0, has_side_effects=True, vmem_limit_bytes=36 << 20
         ),
     )(*[pltpu.with_memory_space_constraint(a, pltpu.HBM) for a in args])
-    outs = pl.pallas_call(
-        store_kernel,
-        out_shape=[jax.ShapeDtypeStruct(s, d) for s, d in shapes],
-        in_specs=[vmem] * 6,
+    sum0, sum1, next0, next1, new0, new1 = pl.pallas_call(
+        finish_kernel,
+        out_shape=[
+            jax.ShapeDtypeStruct((ROWS, WIDE), BF16),
+            jax.ShapeDtypeStruct((ROWS, WIDE), BF16),
+            jax.ShapeDtypeStruct((RANK, WIDE), F32),
+            jax.ShapeDtypeStruct((RANK, WIDE), F32),
+            jax.ShapeDtypeStruct((ROWS, WIDE), F32),
+            jax.ShapeDtypeStruct((ROWS, WIDE), F32),
+        ],
+        in_specs=[vmem] * 4,
         out_specs=[hbm] * 6,
-        scratch_shapes=[dma((6,))],
-        name="store",
-        compiler_params=pltpu.CompilerParams(vmem_limit_bytes=4 << 20),
+        scratch_shapes=[
+            pltpu.VMEM((2, ROWS, WIDE), BF16),
+            pltpu.VMEM((2, RANK, WIDE), F32),
+            dma((10,)),
+        ],
+        name="finish",
+        compiler_params=pltpu.CompilerParams(vmem_limit_bytes=8 << 20),
     )(*held)
-    sum0, sum1, next0, next1, new0, new1 = outs
     return sum0, sum1, next0.T, next1.T, new0[None], new1[None]
 
 

time: 47.2 us -> 45.2 us (0.958)
  Pallas kernels: 46.3 us -> 44.5 us
    pallas_call x2, Pallas kernels: 46.3 us -> 44.5 us  [the longest x1 41.9 us: shards(): pl.pallas_call(main_kernel, out_shape=[pltpu.VMEM((NCH, 2, NX, 8, CH), F3...]
where the time goes in v3:
time: 45.2 us; the launch traced here: 45.1 us
  Pallas kernels  44.5 us (98%)
  between operations  0.64 us (1%)
    pallas_call x1, Pallas kernels, shards(): pl.pallas_call(main_kernel, out_shape=[pltpu.VMEM((NCH, 2, NX, 8, CH), F3...  41.9 us
    pallas_call x1, Pallas kernels, shards(): pl.pallas_call(finish_kernel, out_shape=[jax.ShapeDtypeStruct((ROWS, WIDE...  2.61 us

profile of v3, /device:TPU:8, one launch (start us, length us, event | category | flops | bytes accessed | tf_op | source)
XLA Modules:
  0.0 45.1 jit_solution(8726112331375570662)
XLA Ops:
  0.6 41.9 %compress.1 = (f32[7,2,4,8,256]{4,3,2,1,0:T(8,128)S(1)}, bf16[2,288,96]{2,1,0:T(8,128)(2,1)S(1)}, f32[256,1792]{1,0:T(8,128)S(1)}, f32[256,1792]{1,0:T(8,128)S(1)}) custom-call(bf16[1,256,1792]{2,1,0:T(8,128)(2,1)} %grad0.1, bf16[1,256,1792]{2,1,0:T(8,128)(2,1)} %grad1.1, f32[1,256,1792]{2,1,0:T(8,128)} %error0.1, f32[1,256,1792]{2,1,0:T(8,128)} %error1.1, ...), custom_call_target="tpu_custom_call" | custom-call | tf_op jit(solution)/shard_map/compress/pallas_call | solution.py:337
  42.5 2.6 %finish.1 = (bf16[256,1792]{1,0:T(8,128)(2,1)}, bf16[256,1792]{1,0:T(8,128)(2,1)}, f32[32,1792]{1,0:T(8,128)}, f32[32,1792]{1,0:T(8,128)}, f32[256,1792]{1,0:T(8,128)}, /*index=5*/f32[256,1792]{1,0:T(8,128)}) custom-call(f32[7,2,4,8,256]{4,3,2,1,0:T(8,128)S(1)} %get-tuple-element.16.tsum, bf16[2,288,96]{2,1,0:T(8,128)(2,1)S(1)} %get-tuple-element.17.wide, ...), custom_call_target="tpu_custom_call" | custom-call | tf_op jit(solution)/shard_map/finish/pallas_call | solution.py:353

commit v4 on v3

--- a/solution.py
+++ b/solution.py
@@ -75,9 +75,9 @@
 def main_kernel(
     grad0, grad1, error0, error1, q0, q1,
     tsum, wide, new0, new1,
-    graw, full, qv, fhi, flo, psend, precv, cbuf, zbuf, lmine, left,
+    graw, full, qv, fhi, flo, psend, precv, zbuf, lmine, left,
     tbuf, xr, zs, zr,
-    ldg, lde, ldq, s1, r1, s2, r2, s3, r3, s4, r4,
+    ldg, lde, ldq, s1, r1, s3, r3, s4, r4,
     sx, rx, sz, rz, sgz, rgz, sgx, rgx,
 ):
     grads, errors, qs = (grad0, grad1), (error0, error1), (q0, q1)
@@ -119,7 +119,7 @@
     plane.sort(key=lambda d: -(min(d[0], NX - d[0]) + min(d[1], NY - d[1])))
     column = (4, 3, 5, 2, 6, 1, 7)
     peers = [device(dx=dx, dy=dy) for dx, dy in plane]
-    peers += [device(dc=1)] + [device(dz=k) for k in column]
+    peers += [device(dc=1)] + [device(dz=k, dc=dc) for k in column for dc in range(2)]
     for peer in peers:
         pl.semaphore_signal(barrier, inc=1, device_id=peer, device_id_type=MESH)
 
@@ -166,16 +166,15 @@
     part = psend[mine]
     for k in range(15):
         part += precv[k]
-    cbuf[0] = part
-    send(cbuf.at[0], cbuf.at[1], s2, r2, device(dc=1))
-    wait(cbuf.at[1], r2)
-    zbuf[0] = cbuf[0] + cbuf[1]
+    zbuf[0] = part
     for k in column:
-        send(zbuf.at[0], zbuf.at[k], s3, r3, device(dz=k))
-    wait(zbuf.at[pl.ds(1, 7)], r3)
-    part = zbuf[z]
-    for k in range(1, NZ):
-        part += zbuf[lax.rem(z - k + NZ, NZ)]
+        for dc in (1, 0):
+            send(zbuf.at[0], zbuf.at[2 * k + dc], s3, r3, device(dz=k, dc=dc))
+    send(zbuf.at[0], zbuf.at[1], s3, r3, device(dc=1))
+    wait(zbuf.at[pl.ds(1, 15)], r3)
+    part = zbuf[2 * z + c]
+    for k in range(1, 2 * NZ):
+        part += zbuf[2 * lax.rem(z - k // 2 + NZ, NZ) + lax.rem(c + k, 2)]
     lmine[...] = part
     for dx, dy in plane:
         send(lmine, left.at[mine], s4, r4.at[lax.div(x, 2)], device(dx=dx, dy=dy))
@@ -212,7 +211,7 @@
             zs[b, chunk] = tbuf[chunk, b, x] + xr[chunk, b, 0] + xr[chunk, b, 1] + xr[chunk, b, 2]
 
             def pass_on(b=b, k=k, chunk=chunk, away=away):
-                send(zs.at[b, chunk], zr.at[b, away], sz.at[b, k], rz.at[b], device(dz=away))
+                send(zs.at[b, chunk], zr.at[b, away], sz.at[b, k // 6], rz.at[b], device(dz=away))
 
             if k < NCH - 1:
                 pass_on()
@@ -251,6 +250,21 @@
             cols = slice(j * CH, (j + 1) * CH)
             news[b][:, cols] = full[b, :, cols] - product(wide[b, :ROWS], triple(own), NN)
 
+    wait(precv, s1)
+    wait(zbuf.at[pl.ds(1, 15)], s3)
+    wait(precv, s4)
+    wait(xr, sx)
+    for b in range(2):
+        wait(zs.at[b, pl.ds(0, 6)], sz.at[b, 0])
+
+        @pl.when(z == BARE)
+        def _():
+            wait(zs.at[b, 0], sz.at[b, 1])
+
+        @pl.when(z != BARE)
+        def _():
+            wait(zr.at[b, pl.ds(1, 7)], sgz.at[b])
+
     for b in range(2):
         for k in reversed(range(NCH)):
 
@@ -267,23 +281,7 @@
 
     wait(xr, rgx)
 
-    wait(precv, s1)
-    wait(cbuf.at[1], s2)
-    wait(zbuf.at[pl.ds(1, 7)], s3)
-    wait(precv, s4)
-    wait(xr, sx)
     wait(xr, sgx)
-    for b in range(2):
-        for k in range(NCH - 1):
-            wait(zs.at[b, k], sz.at[b, k])
-
-        @pl.when(z == BARE)
-        def _():
-            wait(zs.at[b, 0], sz.at[b, NCH - 1])
-
-        @pl.when(z != BARE)
-        def _():
-            wait(zr.at[b, pl.ds(1, 7)], sgz.at[b])
 
 
 def finish_kernel(
@@ -321,8 +319,7 @@
         pltpu.VMEM((2, ROWS, WIDE), BF16),
         pltpu.VMEM((16, 8, 128), F32),
         pltpu.VMEM((15, 8, 128), F32),
-        pltpu.VMEM((2, 8, 128), F32),
-        pltpu.VMEM((NZ, 8, 128), F32),
+        pltpu.VMEM((2 * NZ, 8, 128), F32),
         pltpu.VMEM((8, 128), F32),
         pltpu.VMEM((16, 8, 128), F32),
         pltpu.VMEM((NCH, 2, NX, 8, CH), F32),
@@ -330,8 +327,8 @@
         pltpu.VMEM((2, NCH, 8, CH), F32),
         pltpu.VMEM((2, NZ, 8, CH), F32),
         dma((4,)), dma((4,)), dma((2,)),
-        dma, dma, dma, dma, dma, dma, dma, dma((2,)),
-        dma, dma((2, NCH)), dma((2, NCH)), dma((2,)),
+        dma, dma, dma, dma, dma, dma((2,)),
+        dma, dma((2, NCH)), dma((2, 2)), dma((2,)),
         dma((2,)), dma((2, NCH)), dma, dma,
     ]
     held = pl.pallas_call(

time: 45.2 us -> 44.5 us (0.985)
  Pallas kernels: 44.5 us -> 43.8 us
    pallas_call x1, Pallas kernels: 41.9 us -> 41.2 us  [shards(): pl.pallas_call(main_kernel, out_shape=[pltpu.VMEM((NCH, 2, NX, 8, CH), F3...]
where the time goes in v4:
time: 44.5 us; the launch traced here: 44.4 us
  Pallas kernels  43.8 us (98%)
  between operations  0.64 us (1%)
    pallas_call x1, Pallas kernels, shards(): pl.pallas_call(main_kernel, out_shape=[pltpu.VMEM((NCH, 2, NX, 8, CH), F3...  41.2 us
    pallas_call x1, Pallas kernels, shards(): pl.pallas_call(finish_kernel, out_shape=[jax.ShapeDtypeStruct((ROWS, WIDE...  2.61 us

profile of v4, /device:TPU:8, one launch (start us, length us, event | category | flops | bytes accessed | tf_op | source)
XLA Modules:
  0.0 44.4 jit_solution(4892648330982301266)
XLA Ops:
  0.6 41.2 %compress.1 = (f32[7,2,4,8,256]{4,3,2,1,0:T(8,128)S(1)}, bf16[2,288,96]{2,1,0:T(8,128)(2,1)S(1)}, f32[256,1792]{1,0:T(8,128)S(1)}, f32[256,1792]{1,0:T(8,128)S(1)}) custom-call(bf16[1,256,1792]{2,1,0:T(8,128)(2,1)} %grad0.1, bf16[1,256,1792]{2,1,0:T(8,128)(2,1)} %grad1.1, f32[1,256,1792]{2,1,0:T(8,128)} %error0.1, f32[1,256,1792]{2,1,0:T(8,128)} %error1.1, ...), custom_call_target="tpu_custom_call" | custom-call | tf_op jit(solution)/shard_map/compress/pallas_call | solution.py:334
  41.8 2.6 %finish.1 = (bf16[256,1792]{1,0:T(8,128)(2,1)}, bf16[256,1792]{1,0:T(8,128)(2,1)}, f32[32,1792]{1,0:T(8,128)}, f32[32,1792]{1,0:T(8,128)}, f32[256,1792]{1,0:T(8,128)}, /*index=5*/f32[256,1792]{1,0:T(8,128)}) custom-call(f32[7,2,4,8,256]{4,3,2,1,0:T(8,128)S(1)} %get-tuple-element.16.tsum, bf16[2,288,96]{2,1,0:T(8,128)(2,1)S(1)} %get-tuple-element.17.wide, ...), custom_call_target="tpu_custom_call" | custom-call | tf_op jit(solution)/shard_map/finish/pallas_call | solution.py:350

commit v5 on v4

--- a/solution.py
+++ b/solution.py
@@ -101,7 +101,7 @@
     def wait(ref, sem):
         pltpu.make_async_copy(ref, ref, sem).wait()
 
-    groups = [(0, 0, 4), (0, 4, 7), (1, 0, 4), (1, 4, 7)]
+    groups = [(0, 0, 4), (0, 4, 7), (1, 0, 5), (1, 5, 7)]
 
     def load(number):
         b, low, high = groups[number]
@@ -128,7 +128,7 @@
             wait(qv.at[b], ldq.at[b])
             qhi, qlo = split(qv[b])
             both = jnp.concatenate([qhi, qlo], axis=0)
-            acc = jnp.zeros((RANK, ROWS), F32)
+            acc, rest_acc = jnp.zeros((ROWS, 2 * RANK), F32), jnp.zeros((ROWS, RANK), F32)
         cols = pl.ds(low * CH, (high - low) * CH)
         wait(full.at[b, :, cols], lde.at[number])
         wait(graw.at[b, :, cols], ldg.at[number])
@@ -139,10 +139,11 @@
             value = graw[b, :, cols].astype(F32) + full[b, :, cols]
             top, rest = split(value)
             full[b, :, cols], fhi[b, :, cols], flo[b, :, cols] = value, top, rest
-            first = product(both[:, cols], top, NT)
-            acc += first[:RANK] + first[RANK:] + product(qhi[:, cols], rest, NT)
+            acc += product(top, both[:, cols], NT)
+            rest_acc += product(rest, qhi[:, cols], NT)
         if high < NCH:
             continue
+        acc = (acc[:, :RANK] + acc[:, RANK:] + rest_acc).T
         for k in range(8):
             psend[8 * b + k] = acc[8 * (k // 2) : 8 * (k // 2) + 8, 128 * (k % 2) : 128 * (k % 2) + 128]
         if b == 0:
@@ -196,14 +197,18 @@
         lefts.append(jnp.concatenate(rows, axis=0))
         lhi, llo = split(lefts[b])
         both = jnp.concatenate([lhi, llo], axis=0)
-        for chunk, _ in order:
-            cols = pl.ds(pl.multiple_of(chunk * CH, CH), CH)
-            first = product(both, fhi[b, :, cols], NN)
-            value = first[:RANK] + first[RANK:] + product(lhi, flo[b, :, cols], NN)
-            tbuf[chunk, b] = value.reshape(NX, 8, CH)
-            for dx in (2, 1, 3):
-                src = tbuf.at[chunk, b, lax.rem(x + dx, NX)]
-                send(src, xr.at[chunk, b, dx - 1], sx, rx.at[b, chunk], device(dx=dx))
+        for run in ((0,), (1, 2, 3), (4, 5, 6)):
+            for k in run:
+                chunk = order[k][0]
+                cols = pl.ds(pl.multiple_of(chunk * CH, CH), CH)
+                first = product(both, fhi[b, :, cols], NN)
+                value = first[:RANK] + first[RANK:] + product(lhi, flo[b, :, cols], NN)
+                tbuf[chunk, b] = value.reshape(NX, 8, CH)
+            for k in run:
+                chunk = order[k][0]
+                for dx in (2, 1, 3):
+                    src = tbuf.at[chunk, b, lax.rem(x + dx, NX)]
+                    send(src, xr.at[chunk, b, dx - 1], sx, rx.at[b, chunk], device(dx=dx))
 
     for b in range(2):
         for k, (chunk, away) in enumerate(order):
@@ -230,6 +235,13 @@
         wide[b] = jnp.concatenate([top, top, weight - top], axis=0).T.astype(BF16)
 
     for b in range(2):
+
+        if b == 1:
+            for e in range(2):
+                for j in range(NCH):
+                    own = tbuf[j, e].reshape(RANK, CH)
+                    cols = slice(j * CH, (j + 1) * CH)
+                    news[e][:, cols] = full[e, :, cols] - product(wide[e, :ROWS], triple(own), NN)
 
         @pl.when(z != BARE)
         def _():
@@ -239,16 +251,15 @@
                 part += zr[b, k]
             tsum[owned, b, x] = part
             here = tsum.at[owned, b, x]
-            for k in column:
-                send(here, here, sgz.at[b], rgz.at[b, owned], device(dz=k))
+            for place in (0, 1, 2, 3, 7, 6, 5, 4):
+
+                @pl.when(z != place)
+                def _():
+                    to = (place * NX + x, tensor)
+                    send(here, here, sgz.at[b], rgz.at[b, owned], to)
+
             for dx in (2, 1, 3):
                 send(here, here, sgx, rgx, device(dx=dx))
-
-    for b in range(2):
-        for j in range(NCH):
-            own = tbuf[j, b].reshape(RANK, CH)
-            cols = slice(j * CH, (j + 1) * CH)
-            news[b][:, cols] = full[b, :, cols] - product(wide[b, :ROWS], triple(own), NN)
 
     wait(precv, s1)
     wait(zbuf.at[pl.ds(1, 15)], s3)

time: 44.5 us -> 44.5 us (level)
  no operation moved by 1% of the time
where the time goes in v5:
time: 44.5 us; the launch traced here: 44.4 us
  Pallas kernels  43.7 us (98%)
  between operations  0.64 us (1%)
    pallas_call x1, Pallas kernels, shards(): pl.pallas_call(main_kernel, out_shape=[pltpu.VMEM((NCH, 2, NX, 8, CH), F3...  41.1 us
    pallas_call x1, Pallas kernels, shards(): pl.pallas_call(finish_kernel, out_shape=[jax.ShapeDtypeStruct((ROWS, WIDE...  2.61 us

profile of v5, /device:TPU:8, one launch (start us, length us, event | category | flops | bytes accessed | tf_op | source)
XLA Modules:
  0.0 44.4 jit_solution(7625275152866941299)
XLA Ops:
  0.6 41.1 %compress.1 = (f32[7,2,4,8,256]{4,3,2,1,0:T(8,128)S(1)}, bf16[2,288,96]{2,1,0:T(8,128)(2,1)S(1)}, f32[256,1792]{1,0:T(8,128)S(1)}, f32[256,1792]{1,0:T(8,128)S(1)}) custom-call(bf16[1,256,1792]{2,1,0:T(8,128)(2,1)} %grad0.1, bf16[1,256,1792]{2,1,0:T(8,128)(2,1)} %grad1.1, f32[1,256,1792]{2,1,0:T(8,128)} %error0.1, f32[1,256,1792]{2,1,0:T(8,128)} %error1.1, ...), custom_call_target="tpu_custom_call" | custom-call | tf_op jit(solution)/shard_map/compress/pallas_call | solution.py:345
  41.8 2.6 %finish.1 = (bf16[256,1792]{1,0:T(8,128)(2,1)}, bf16[256,1792]{1,0:T(8,128)(2,1)}, f32[32,1792]{1,0:T(8,128)}, f32[32,1792]{1,0:T(8,128)}, f32[256,1792]{1,0:T(8,128)}, /*index=5*/f32[256,1792]{1,0:T(8,128)}) custom-call(f32[7,2,4,8,256]{4,3,2,1,0:T(8,128)S(1)} %get-tuple-element.16.tsum, bf16[2,288,96]{2,1,0:T(8,128)(2,1)S(1)} %get-tuple-element.17.wide, ...), custom_call_target="tpu_custom_call" | custom-call | tf_op jit(solution)/shard_map/finish/pallas_call | solution.py:361
